TPU v7x, 32 devices: a whole 2x2x4 slice. The times are simulated.
32 devices in a mesh: groups: 2 (over x), tensor: 16 (over z, y, core).
Axes of the slice: x: 2, y: 2, z: 4, core: 2. Of those that a mesh axis runs over, the one named last changes fastest.
Arguments:
- tokens_in: bfloat16 [1024, 8192], P(('groups', 'tensor')), parts along dimension 0, may hold values from -4 to 4
- mask_pos: int32 [4, 64], P('groups'), parts along dimension 0, may hold values from 0 to 255
- step_index: int32 [4], P('groups'), parts along dimension 0, may hold values from 0 to 63
- mask_embed: bfloat16 [8192], replicated, may hold values from -5 to 5
- time_table: bfloat16 [64, 8192], replicated, may hold values from -4 to 4
- norm_gain: float32 [8192], replicated, may hold values from 0.5 to 1.5
- w_qkv: bfloat16 [3, 8192, 2048], P(None, None, 'tensor'), may hold values from -0.0625 to 0.0625
- qk_gain: float32 [2, 2048], P(None, 'tensor'), may hold values from 1 to 2
- w_out: bfloat16 [2048, 8192], P('tensor'), may hold values from -0.5 to 0.5
Outputs:
- mixed: bfloat16 [1024, 8192], P('groups', 'tensor'), parts along dimension 0
There are 2 independent parts, one for each index of `groups`. A program takes and returns all parts, laid end to end along the dimension named above; an argument that names none is the same for every part. Nothing has to cross between parts.
Inputs may be any that keep to these rules, and one draw needn't show every extreme that they name: `mask_pos`: listed positions may repeat; a position is masked if it is listed at least once.
All inputs are finite; a program needn't handle non-finite values.
Results may differ from a plain program's by a relative error of at most 0.007.
Values may be sent and summed in bfloat16 or wider, within the bound.
A program may use at most 128 MiB of HBM per device.

v0:
```python
import jax
import jax.numpy as jnp
from jax import lax
from jax.sharding import PartitionSpec as P

HEAD_DIM = 128
SEQS = 2
LEN = 256
STEPS = 64


def embed_rows(rows_tokens, row_ids, mask_pos, step_index, mask_part, table_part):
    seq_of = row_ids // LEN
    pos_of = row_ids % LEN
    seq_range = jnp.arange(SEQS, dtype=jnp.int32)
    listed = (mask_pos[None, :, :] == pos_of[:, None, None]) & (
        seq_range[None, :, None] == seq_of[:, None, None]
    )
    masked = jnp.any(listed, axis=(1, 2))
    step_row = jnp.sum(
        jnp.where(seq_range[None, :] == seq_of[:, None], step_index[None, :], 0), axis=1
    )
    onehot = (step_row[:, None] == jnp.arange(STEPS, dtype=jnp.int32)[None, :]).astype(jnp.bfloat16)
    timed = jnp.dot(onehot, table_part, preferred_element_type=jnp.float32)
    base = jnp.where(
        masked[:, None], mask_part[None, :].astype(jnp.float32), rows_tokens.astype(jnp.float32)
    )
    return base + timed


def attend(qkv, gains):
    query = qkv[:, 0]
    keys = qkv[:, 1]
    query_n = (
        query * lax.rsqrt(jnp.mean(query * query, axis=-1, keepdims=True) + 1e-06) * gains[0]
    ).astype(jnp.bfloat16)
    keys_n = (
        keys * lax.rsqrt(jnp.mean(keys * keys, axis=-1, keepdims=True) + 1e-06) * gains[1]
    ).astype(jnp.bfloat16)
    values = qkv[:, 2].astype(jnp.bfloat16)
    width = qkv.shape[-1]
    query_n = query_n.reshape(SEQS, LEN, width)
    keys_n = keys_n.reshape(SEQS, LEN, width)
    values = values.reshape(SEQS, LEN, width)
    scores = jnp.einsum(
        "sqh,skh->sqk", query_n, keys_n, preferred_element_type=jnp.float32
    ) / jnp.sqrt(jnp.float32(width))
    weights = jnp.exp(scores)
    probs = (weights / jnp.sum(weights, axis=-1, keepdims=True)).astype(jnp.bfloat16)
    attn = jnp.einsum("sqk,skh->sqh", probs, values, preferred_element_type=jnp.float32)
    return attn.reshape(SEQS * LEN, width).astype(jnp.bfloat16)


def body(tokens_in, mask_pos, step_index, mask_embed, time_table, norm_gain, w_qkv, qk_gain, w_out):
    rows_here = tokens_in.shape[0]
    my_index = lax.axis_index("tensor")
    col_count = tokens_in.shape[1] // lax.axis_size("tensor")
    local_ids = my_index * rows_here + jnp.arange(rows_here, dtype=jnp.int32)
    embedded_rows = embed_rows(tokens_in, local_ids, mask_pos, step_index, mask_embed, time_table)
    normed = (
        embedded_rows
        * lax.rsqrt(jnp.mean(embedded_rows * embedded_rows, axis=-1, keepdims=True) + 1e-05)
        * norm_gain
    ).astype(jnp.bfloat16)
    qkv = jnp.einsum(
        "td,cdh->tch",
        lax.all_gather(normed, "tensor", axis=0, tiled=True),
        w_qkv,
        preferred_element_type=jnp.float32,
    )
    total_rows = qkv.shape[0]
    heads_here = qkv.shape[2] // HEAD_DIM
    qkv_heads = qkv.reshape(total_rows, 3, heads_here, HEAD_DIM)
    gains_heads = qk_gain.reshape(2, heads_here, HEAD_DIM)
    attn = jax.vmap(attend, in_axes=(2, 1), out_axes=1)(qkv_heads, gains_heads)
    attn = attn.reshape(total_rows, heads_here * HEAD_DIM)
    col_tokens = lax.all_to_all(tokens_in, "tensor", split_axis=1, concat_axis=0, tiled=True)
    col_start = my_index * col_count
    mask_part = lax.dynamic_slice_in_dim(mask_embed, col_start, col_count, 0)
    table_part = lax.dynamic_slice_in_dim(time_table, col_start, col_count, 1)
    all_ids = jnp.arange(total_rows, dtype=jnp.int32)
    embedded_cols = embed_rows(col_tokens, all_ids, mask_pos, step_index, mask_part, table_part)
    partial_terms = jnp.dot(attn, w_out, preferred_element_type=jnp.float32)
    branch = lax.psum_scatter(partial_terms, "tensor", scatter_dimension=1, tiled=True)
    return (embedded_cols + branch).astype(jnp.bfloat16)


def solution(mesh):
    return jax.shard_map(
        body,
        mesh=mesh,
        in_specs=(
            P(("groups", "tensor"), None),
            P("groups", None),
            P("groups"),
            P(),
            P(),
            P(),
            P(None, None, "tensor"),
            P(None, "tensor"),
            P("tensor", None),
        ),
        out_specs=P("groups", "tensor"),
        check_vma=False,
    )
```

profile of v0, /device:TPU:0, one launch (start us, length us, event | category | flops | bytes accessed | tf_op | source)
XLA Modules:
  0.0 294.6 jit_solution(13188922312778145624)
XLA Ops:
  6.6 0.9 select_reduce_fusion.1
  7.5 0.7 convert_element_type.67
  8.2 0.9 and_reduce_fusion.1
  9.0 1.9 multiply_reduce_fusion
  10.9 1.7 multiply_convert_fusion
  12.7 0.0 all-gather.2.cloned.1.call-update
  12.7 0.0 reduce-scatter.2.cloned.1.call-start
  12.7 0.8 slice_bitcast_fusion.1
  13.5 76.9 %all-gather.2.cloned.1.call-done = bf16[512,8192]{1,0:T(8,128)(2,1)} async-done(((bf16[32,8192]{1,0:T(8,128)(2,1)}), bf16[512,8192]{1,0:T(8,128)(2,1)}) %all-gather.2.cloned.1.call-update) | async-done | bytes 8388624 | tf_op jit(solution)/shard_map/all_gather | solution.py:67
  90.4 8.9 %fusion.3 = f32[512,3,1,128]{3,0,1,2:T(8,128)S(1)} fusion(bf16[3,8192,128]{2,1,0:T(8,128)(2,1)} %param.15, bf16[512,8192]{1,0:T(8,128)(2,1)} %all-gather.2.cloned.1.call-done), kind=kOutput, calls=%fused_computation.5 | convolution fusion | flops 3221225472 | bytes 15466496 | tf_op jit(solution)/shard_map/td,cdh->tch/dot_general | solution.py:65
  99.3 0.2 multiply_reduce_fusion.2
  99.6 0.4 fusion.7
  100.0 0.3 convolution_convert_fusion
  100.3 8.1 %fusion.23 = f32[512,8192]{1,0:T(8,128)} fusion(bf16[512,128]{1,0:T(8,128)(2,1)S(1)} %bitcast.32, bf16[128,8192]{1,0:T(8,128)(2,1)S(1)} %copy-done), kind=kOutput, calls=%fused_computation.60 | convolution fusion | flops 1073741824 | bytes 19005440 | tf_op jit(solution)/shard_map/dot_general | solution.py:83
  108.4 1.0 copy-done.1
  109.4 0.8 copy.17
  110.3 4.2 %all-to-all-start = ((bf16[32,16,512]{2,0,1:T(8,128)(2,1)}), bf16[32,16,512]{2,0,1:T(8,128)(2,1)}, u32[]{:S(2)}, u32[]{:S(2)}) async-start(bf16[32,16,512]{2,0,1:T(8,128)(2,1)} %bitcast.28), calls=%async_computation | async-start | bytes 1048576 | tf_op jit(solution)/shard_map/all_to_all | solution.py:77
  114.5 0.8 dynamic-slice_convert_fusion
  115.3 0.1 select_reduce_fusion
  115.4 0.1 and_reduce_fusion
  115.5 13.5 %all-to-all-done = bf16[32,16,512]{2,0,1:T(8,128)(2,1)} async-done(((bf16[32,16,512]{2,0,1:T(8,128)(2,1)}), bf16[32,16,512]{2,0,1:T(8,128)(2,1)}, u32[]{:S(2)}, u32[]{:S(2)}) %all-to-all-start) | async-done | bytes 524320 | tf_op jit(solution)/shard_map/all_to_all | solution.py:77
  129.0 1.3 bitcast_select_fusion
  130.2 155.1 %reduce-scatter.2.cloned.1.call-done = f32[512,512]{1,0:T(8,128)} async-done(((f32[512,8192]{1,0:T(8,128)}), f32[512,512]{1,0:T(8,128)}) %reduce-scatter.2.cloned.1.call-update) | async-done | bytes 1048592 | tf_op jit(solution)/shard_map/reduce_scatter | solution.py:84
  285.3 2.4 fusion.6
  (20 shorter events, 0.1 us)
Async XLA Ops:
  6.5 93.8 %copy-start = (bf16[128,8192]{1,0:T(8,128)(2,1)S(1)}, bf16[128,8192]{1,0:T(8,128)(2,1)}, u32[]{:S(2)}) copy-start(bf16[128,8192]{1,0:T(8,128)(2,1)} %param.17) | copy-start | bytes 6291460
  6.5 83.9 %all-gather.2.cloned.1.call-start = ((), (), s32[]{:S(2)}) async-start(), calls=%async_computation.2 | async-start | bytes 8912896 | tf_op jit(solution)/shard_map/all_gather | solution.py:67
  12.7 272.7 %reduce-scatter.2.cloned.1.call-start = ((), (), s32[]{:S(2)}) async-start(), calls=%async_computation.3 | async-start | bytes 17825792 | tf_op jit(solution)/shard_map/reduce_scatter | solution.py:84
  108.4 1.0 copy-start.1
  108.4 6.9 %copy-start.3 = (s32[2]{0:T(128)S(1)}, s32[2]{0:T(128)}, u32[]{:S(2)}) copy-start(s32[2]{0:T(128)} %param.11) | copy-start | bytes 28
  108.4 7.0 %copy-start.2 = (s32[2,64]{1,0:T(2,128)S(1)}, s32[2,64]{1,0:T(2,128)}, u32[]{:S(2)}) copy-start(s32[2,64]{1,0:T(2,128)} %param.10) | copy-start | bytes 1540
  110.3 18.7 %all-to-all-start = ((bf16[32,16,512]{2,0,1:T(8,128)(2,1)}), bf16[32,16,512]{2,0,1:T(8,128)(2,1)}, u32[]{:S(2)}, u32[]{:S(2)}) async-start(bf16[32,16,512]{2,0,1:T(8,128)(2,1)} %bitcast.28), calls=%async_computation | async-start | bytes 1048576 | tf_op jit(solution)/shard_map/all_to_all | solution.py:77
Sparse Core Ops, SparseCore 0:
  12.8 77.5 all-gather.1
  108.5 176.7 reduce-scatter.1
where the time goes:
time: 295 us
  waiting for transfers between devices  246 us (83%)
  matrix products  21.9 us (7%)
  between operations  13.5 us (5%)
  other arithmetic  6.69 us (2%)
  starting transfers between devices  4.28 us (1%)
    reduce_scatter x1, waiting for transfers between devices, body(): lax.psum_scatter(partial_terms, 'tensor', scatter_dimension=1, tiled=True)  155 us
    all_gather x1, waiting for transfers between devices, body(): lax.all_gather(normed, 'tensor', axis=0, tiled=True)  76.9 us
    all_to_all x1, waiting for transfers between devices, body(): lax.all_to_all(tokens_in, 'tensor', split_axis=1, concat_axis=0, tiled=True)  13.5 us
    dot_general x1, matrix products, body(): jnp.einsum('td,cdh->tch', lax.all_gather(normed, 'tensor', axis=0, tiled=...  8.88 us
    dot_general x1, matrix products, body(): partial_terms = jnp.dot(attn, w_out, preferred_element_type=jnp.float32)  8.06 us
  transfers between devices with their start and end apart: 3, of which 3 were waited for; matrix products, arithmetic and copies ran while one was open for 1% of the time, Pallas kernels for 0%

commit v1 on v0

--- a/solution.py
+++ b/solution.py
@@ -52,36 +52,35 @@
 
 
 def body(tokens_in, mask_pos, step_index, mask_embed, time_table, norm_gain, w_qkv, qk_gain, w_out):
-    rows_here = tokens_in.shape[0]
     my_index = lax.axis_index("tensor")
     col_count = tokens_in.shape[1] // lax.axis_size("tensor")
-    local_ids = my_index * rows_here + jnp.arange(rows_here, dtype=jnp.int32)
-    embedded_rows = embed_rows(tokens_in, local_ids, mask_pos, step_index, mask_embed, time_table)
+    w_cols = lax.all_to_all(w_out, "tensor", split_axis=1, concat_axis=0, tiled=True)
+    tokens = lax.all_gather(tokens_in, "tensor", axis=0, tiled=True)
+    total_rows = tokens.shape[0]
+    all_ids = jnp.arange(total_rows, dtype=jnp.int32)
+    embedded = embed_rows(tokens, all_ids, mask_pos, step_index, mask_embed, time_table)
     normed = (
-        embedded_rows
-        * lax.rsqrt(jnp.mean(embedded_rows * embedded_rows, axis=-1, keepdims=True) + 1e-05)
+        embedded
+        * lax.rsqrt(jnp.mean(embedded * embedded, axis=-1, keepdims=True) + 1e-05)
         * norm_gain
     ).astype(jnp.bfloat16)
-    qkv = jnp.einsum(
-        "td,cdh->tch",
-        lax.all_gather(normed, "tensor", axis=0, tiled=True),
-        w_qkv,
-        preferred_element_type=jnp.float32,
-    )
-    total_rows = qkv.shape[0]
+    qkv = jnp.einsum("td,cdh->tch", normed, w_qkv, preferred_element_type=jnp.float32)
     heads_here = qkv.shape[2] // HEAD_DIM
     qkv_heads = qkv.reshape(total_rows, 3, heads_here, HEAD_DIM)
     gains_heads = qk_gain.reshape(2, heads_here, HEAD_DIM)
     attn = jax.vmap(attend, in_axes=(2, 1), out_axes=1)(qkv_heads, gains_heads)
     attn = attn.reshape(total_rows, heads_here * HEAD_DIM)
-    col_tokens = lax.all_to_all(tokens_in, "tensor", split_axis=1, concat_axis=0, tiled=True)
+    attn_all = lax.all_gather(attn, "tensor", axis=1, tiled=True)
     col_start = my_index * col_count
-    mask_part = lax.dynamic_slice_in_dim(mask_embed, col_start, col_count, 0)
-    table_part = lax.dynamic_slice_in_dim(time_table, col_start, col_count, 1)
-    all_ids = jnp.arange(total_rows, dtype=jnp.int32)
-    embedded_cols = embed_rows(col_tokens, all_ids, mask_pos, step_index, mask_part, table_part)
-    partial_terms = jnp.dot(attn, w_out, preferred_element_type=jnp.float32)
-    branch = lax.psum_scatter(partial_terms, "tensor", scatter_dimension=1, tiled=True)
+    embedded_cols = embed_rows(
+        lax.dynamic_slice_in_dim(tokens, col_start, col_count, 1),
+        all_ids,
+        mask_pos,
+        step_index,
+        lax.dynamic_slice_in_dim(mask_embed, col_start, col_count, 0),
+        lax.dynamic_slice_in_dim(time_table, col_start, col_count, 1),
+    )
+    branch = jnp.dot(attn_all, w_cols, preferred_element_type=jnp.float32)
     return (embedded_cols + branch).astype(jnp.bfloat16)
 
 

time: 295 us -> 196 us (0.66)
  waiting for transfers between devices: 246 us -> 139 us
  local copies, waits for them, and re-layouts: 2.68 us -> 8.03 us
  other arithmetic: 6.69 us -> 2.39 us
  starting transfers between devices: 4.28 us -> 7.46 us
    reduce_scatter x1 -> x0, waiting for transfers between devices: 155 us -> none  [body(): lax.psum_scatter(partial_terms, 'tensor', scatter_dimension=1, tiled=True)]
    all_gather x1 -> x2, waiting for transfers between devices: 76.9 us -> 138 us  [the longest x1 102 us: body(): tokens = lax.all_gather(tokens_in, 'tensor', axis=0, tiled=True)]
    all_to_all x1, waiting for transfers between devices: 13.5 us -> 0.01 us  [body(): lax.all_to_all(w_out, 'tensor', split_axis=1, concat_axis=0, tiled=True)]
    dot_general x2, matrix products: 16.9 us -> 11.8 us  [the longest x1 8.28 us: body(): jnp.einsum('td,cdh->tch', normed, w_qkv, preferred_element_type=jnp.float32)]
    dot_general x2, matrix products: 4.28 us -> 8.56 us  [embed_rows(): timed = jnp.dot(onehot, table_part, preferred_element_type=jnp.float32)]
    all_to_all x1, starting transfers between devices: 4.24 us -> 7.39 us  [body(): lax.all_to_all(w_out, 'tensor', split_axis=1, concat_axis=0, tiled=True)]
    unnamed x8 -> x13, local copies, waits for them, and re-layouts: 1.02 us -> 4.09 us
  transfers between devices with their start and end apart: 3 -> 3, of which waited for: 3 -> 2; matrix products, arithmetic and copies ran while one was open for 1% -> 15% of each run, Pallas kernels for 0% -> 0%
where the time goes in v1:
time: 196 us; the launch traced here: 195 us
  waiting for transfers between devices  139 us (71%)
  matrix products  24.6 us (13%)
  between operations  13.5 us (7%)
  local copies, waits for them, and re-layouts  8.03 us (4%)
  starting transfers between devices  7.46 us (4%)
  other arithmetic  2.39 us (1%)
    all_gather x1, waiting for transfers between devices, body(): tokens = lax.all_gather(tokens_in, 'tensor', axis=0, tiled=True)  102 us
    all_gather x1, waiting for transfers between devices, body(): attn_all = lax.all_gather(attn, 'tensor', axis=1, tiled=True)  36.9 us
    dot_general x2, matrix products, embed_rows(): timed = jnp.dot(onehot, table_part, preferred_element_type=jnp.float32)  8.56 us
    dot_general x1, matrix products, body(): jnp.einsum('td,cdh->tch', normed, w_qkv, preferred_element_type=jnp.float32)  8.28 us
    all_to_all x1, starting transfers between devices, body(): lax.all_to_all(w_out, 'tensor', split_axis=1, concat_axis=0, tiled=True)  7.39 us
    unnamed x13, local copies, waits for them, and re-layouts  4.09 us
  transfers between devices with their start and end apart: 3, of which 2 were waited for; matrix products, arithmetic and copies ran while one was open for 15% of the time, Pallas kernels for 0%

profile of v1, /device:TPU:0, one launch (start us, length us, event | category | flops | bytes accessed | tf_op | source)
XLA Modules:
  0.0 195.2 jit_solution(3192070384309552772)
XLA Ops:
  6.5 0.0 copy-start
  6.5 0.0 all-gather.3.cloned.1.call-start
  6.6 0.7 all-gather.3.cloned.1.call-update
  7.3 4.1 %copy.16 = bf16[128,8192]{0,1:T(8,128)(2,1)} copy(bf16[128,8192]{1,0:T(8,128)(2,1)} %param.17) | data formatting | bytes 4194304 | tf_op args[8]
  11.4 7.4 %all-to-all-start = ((bf16[128,16,512]{0,2,1:T(8,128)(2,1)}), bf16[128,16,512]{0,2,1:T(8,128)(2,1)S(1)}, u32[]{:S(2)}, u32[]{:S(2)}) async-start(bf16[128,16,512]{0,2,1:T(8,128)(2,1)} %bitcast.25), calls=%async_computation | async-start | bytes 4194304 | tf_op jit(solution)/shard_map/all_to_all | solution.py:57
  18.7 0.0 all-gather.5.cloned.1.call-start
  18.9 0.1 select_reduce_fusion
  18.9 0.1 and_reduce_fusion
  19.1 0.6 slice_bitcast_fusion.1
  19.7 101.6 %all-gather.3.cloned.1.call-done = bf16[512,8192]{1,0:T(8,128)(2,1)} async-done(((bf16[32,8192]{1,0:T(8,128)(2,1)}), bf16[512,8192]{1,0:T(8,128)(2,1)}) %all-gather.3.cloned.1.call-update) | async-done | bytes 8388624 | tf_op jit(solution)/shard_map/all_gather | solution.py:58
  121.2 6.4 %multiply_reduce_fusion = (f32[512]{0:T(512)S(1)}, f32[512,8192]{1,0:T(8,128)S(1)}) fusion(bf16[64,8192]{1,0:T(8,128)(2,1)S(1)} %copy-done, s32[512]{0:T(512)S(1)} %select_reduce_fusion, bf16[512,8192]{1,0:T(8,128)(2,1)} %all-gather.3.cloned.1.call-done, f32[8192]{0:T(1024)S(1)} %convert_element_type.59, pred[512]{0:T(512)(128)(4,1)S(1)} %and_reduce_fusion), kind=kOutput, calls=%fused_computation.1 | convolution fusion | flops 557874688 | bytes 26251776 | tf_op jit(solution)/shard_map/dot_general | solution.py:24
  127.6 8.3 %fusion.7 = f32[512,3,1,128]{3,0,1,2:T(8,128)S(1)} fusion(bf16[3,8192,128]{2,1,0:T(8,128)(2,1)} %param.15, f32[512,8192]{1,0:T(8,128)S(1)} %get-tuple-element.12, f32[8192]{0:T(1024)S(1)} %copy-done.5, f32[512]{0:T(512)S(1)} %add_rsqrt_fusion.2), kind=kOutput, calls=%fused_computation.10 | convolution fusion | flops 3233808384 | bytes 23889920 | tf_op jit(solution)/shard_map/td,cdh->tch/dot_general | solution.py:67
  135.9 0.8 multiply_reduce_fusion.2
  136.8 0.6 add_rsqrt_fusion
  137.4 0.7 rsqrt.34
  138.1 2.1 %fusion.10 = f32[2,256,256]{1,2,0:T(8,128)} fusion(f32[2,256,128]{2,1,0:T(8,128)} %bitcast.28, f32[2,256,128]{2,1,0:T(8,128)S(1)} %bitcast.27, f32[128]{0:T(128)} %get-tuple-element.10, f32[2,256]{1,0:T(2,128)S(1)} %rsqrt.34, f32[128]{0:T(128)} %get-tuple-element.9, f32[2,256]{1,0:T(2,128)S(1)} %rsqrt.32), kind=kOutput, calls=%fused_computation.12 | convolution fusion | flops 34078720 | bytes 1053696 | tf_op jit(solution)/shard_map/vmap(sqh,skh->sqk)/dot_general | solution.py:45
  140.2 2.2 %convolution_convert_fusion = bf16[2,256,128]{2,1,0:T(8,128)(2,1)} fusion(bf16[2,256,128]{2,1,0:T(8,128)(2,1)S(1)} %bitcast.30, f32[2,256,256]{1,2,0:T(8,128)} %fusion.10), kind=kOutput, calls=%fused_computation.13 | convolution fusion | flops 33882880 | bytes 786432 | tf_op jit(solution)/shard_map/vmap(sqk,skh->sqh)/dot_general | solution.py:50
  142.3 0.0 all-gather.5.cloned.1.call-update
  142.4 0.8 dynamic-slice_convert_fusion
  143.1 0.0 all-to-all-done
  143.1 2.6 %copy.17 = bf16[16,128,512]{2,1,0:T(8,128)(2,1)} copy(bf16[16,128,512]{1,2,0:T(8,128)(2,1)S(1)} %bitcast.24) | data formatting | bytes 4194304 | tf_op jit(solution)/shard_map/all_to_all | solution.py:57
  145.8 36.9 %all-gather.5.cloned.1.call-done = bf16[512,2048]{1,0:T(8,128)(2,1)} async-done(((bf16[512,128]{1,0:T(8,128)(2,1)}), bf16[512,2048]{1,0:T(8,128)(2,1)}) %all-gather.5.cloned.1.call-update) | async-done | bytes 2097168 | tf_op jit(solution)/shard_map/all_gather | solution.py:73
  182.6 3.5 %fusion.26 = f32[512,512]{1,0:T(8,128)S(1)} fusion(bf16[512,2048]{1,0:T(8,128)(2,1)} %all-gather.5.cloned.1.call-done, bf16[2048,512]{1,0:T(8,128)(2,1)} %bitcast.26), kind=kOutput, calls=%fused_computation.50 | convolution fusion | flops 1073741824 | bytes 5242880 | tf_op jit(solution)/shard_map/dot_general | solution.py:83
  186.1 2.2 %fusion.6 = bf16[512,512]{1,0:T(8,128)(2,1)} fusion(f32[512,512]{1,0:T(8,128)S(1)} %fusion.26, bf16[512,8192]{1,0:T(8,128)(2,1)} %all-gather.3.cloned.1.call-done, s32[]{:T(128)S(6)} %select_n.49, f32[512]{0:T(512)S(1)} %dynamic-slice_convert_fusion, pred[512]{0:T(512)(128)(4,1)S(1)} %and_reduce_fusion, s32[512]{0:T(512)S(1)} %select_reduce_fusion, ...), kind=kOutput, calls=%fused_computation.9 | convolution fusion | flops 34897920 | bytes 2168320 | tf_op jit(solution)/shard_map/dot_general | solution.py:24
  (18 shorter events, 0.1 us)
Async XLA Ops:
  6.5 114.7 %copy-start = (bf16[64,8192]{1,0:T(8,128)(2,1)S(1)}, bf16[64,8192]{1,0:T(8,128)(2,1)}, u32[]{:S(2)}) copy-start(bf16[64,8192]{1,0:T(8,128)(2,1)} %param.13) | copy-start | bytes 3145732
  6.5 12.3 %copy-start.1 = (bf16[8192]{0:T(1024)(128)(2,1)S(1)}, bf16[8192]{0:T(1024)(128)(2,1)}, u32[]{:S(2)}) copy-start(bf16[8192]{0:T(1024)(128)(2,1)} %param.12) | copy-start | bytes 49156
  6.5 12.3 %copy-start.4 = (s32[2]{0:T(128)S(1)}, s32[2]{0:T(128)}, u32[]{:S(2)}) copy-start(s32[2]{0:T(128)} %param.11) | copy-start | bytes 28
  6.5 12.4 %copy-start.3 = (s32[2,64]{1,0:T(2,128)S(1)}, s32[2,64]{1,0:T(2,128)}, u32[]{:S(2)}) copy-start(s32[2,64]{1,0:T(2,128)} %param.10) | copy-start | bytes 1540
  6.5 12.5 %copy-start.2 = (f32[2,128]{1,0:T(2,128)S(1)}, f32[2,128]{1,0:T(2,128)}, u32[]{:S(2)}) copy-start(f32[2,128]{1,0:T(2,128)} %param.16) | copy-start | bytes 3076
  6.5 114.7 %all-gather.3.cloned.1.call-start = ((), (), s32[]{:S(2)}) async-start(), calls=%async_computation.1 | async-start | bytes 8912896 | tf_op jit(solution)/shard_map/all_gather | solution.py:58
  11.4 131.8 %all-to-all-start = ((bf16[128,16,512]{0,2,1:T(8,128)(2,1)}), bf16[128,16,512]{0,2,1:T(8,128)(2,1)S(1)}, u32[]{:S(2)}, u32[]{:S(2)}) async-start(bf16[128,16,512]{0,2,1:T(8,128)(2,1)} %bitcast.25), calls=%async_computation | async-start | bytes 4194304 | tf_op jit(solution)/shard_map/all_to_all | solution.py:57
  18.7 163.9 %all-gather.5.cloned.1.call-start = ((), (), s32[]{:S(2)}) async-start(), calls=%async_computation.2 | async-start | bytes 2228224 | tf_op jit(solution)/shard_map/all_gather | solution.py:73
  19.7 108.0 %copy-start.5 = (f32[8192]{0:T(1024)S(1)}, f32[8192]{0:T(1024)}, u32[]{:S(2)}) copy-start(f32[8192]{0:T(1024)} %param.14) | copy-start | bytes 98308
Sparse Core Ops, SparseCore 0:
  9.5 111.6 all-gather.2
  142.5 40.0 all-gather.4

commit v2 on v1

--- a/solution.py
+++ b/solution.py
@@ -1,6 +1,8 @@
 import jax
 import jax.numpy as jnp
 from jax import lax
+from jax.experimental import pallas as pl
+from jax.experimental.pallas import tpu as pltpu
 from jax.sharding import PartitionSpec as P
 
 HEAD_DIM = 128
@@ -84,9 +86,380 @@
     return (embedded_cols + branch).astype(jnp.bfloat16)
 
 
+MESH = pl.DeviceIdType.MESH
+NZ = 4
+NY = 2
+CHUNK = 1024
+
+
+def fused_kernel(
+    tok, mpos, step, membed, table, ngain, wqkv, qkg, wout, out,
+    xall, wv, wcols, tsc, qkv, att, acc,
+    loc, recv, send_z, send_y, send_s, wsend, wrecv, wx, arecv, asend_z, asend_y, asend_s,
+):
+    n, rows, width = xall.shape
+    cols = width // n
+    me = lax.axis_index("tensor")
+    grp = lax.axis_index("groups")
+    core = me % 2
+    y = (me // 2) % NY
+    z = me // (2 * NY)
+    far = z // 2
+    zlist = [z, 2 * far + 1 - z % 2, 2 - far, 3 - 3 * far]
+
+    def index(zz, yy, cc):
+        return (zz * NY + yy) * 2 + cc
+
+    sibling = index(z, y, 1 - core)
+    across = index(z, 1 - y, core)
+
+    own = pltpu.make_async_copy(tok, xall.at[me], loc.at[0])
+    own.start()
+    wcopies = [
+        pltpu.make_async_copy(wqkv.at[c], wv.at[:, pl.ds(c * HEAD_DIM, HEAD_DIM)], loc.at[1 + c]) for c in range(3)
+    ]
+    for c in wcopies:
+        c.start()
+    half = wout.shape[0] // 2
+    wrows = pl.ds(pl.multiple_of(grp * half, half), half)
+
+    def wblock(d):
+        return wout.at[wrows, pl.ds(pl.multiple_of(d * cols, cols), cols)]
+
+    wown = pltpu.make_async_copy(wblock(me), wcols.at[me, grp], loc.at[4])
+    wown.start()
+
+    barrier = pltpu.get_barrier_semaphore()
+
+    def greet(i, carry):
+        pl.semaphore_signal(barrier, inc=1, device_id={"tensor": (me + i) % n}, device_id_type=MESH)
+        return carry
+
+    lax.fori_loop(1, n, greet, 0)
+    pl.semaphore_signal(barrier, inc=1, device_id={"groups": 1 - grp}, device_id_type=MESH)
+    pl.semaphore_wait(barrier, n)
+
+    def relay(buf, rsem, sz, sy, ss):
+        def copy(src, j, sem, to):
+            return pltpu.make_async_remote_copy(
+                src_ref=src, dst_ref=buf.at[j], send_sem=sem, recv_sem=rsem.at[j],
+                device_id={"tensor": to}, device_id_type=MESH,
+            )
+
+        def arrived(j):
+            copy(buf.at[j], j, sy.at[0], sibling).wait_recv()
+
+        def start_own(src):
+            @pl.when(z < NZ - 1)
+            def _():
+                copy(src, me, sz.at[0], me + 2 * NY).start()
+
+            @pl.when(z > 0)
+            def _():
+                copy(src, me, sz.at[4], me - 2 * NY).start()
+
+            copy(src, me, sy.at[0], across).start()
+            copy(src, me, ss.at[0], sibling).start()
+
+        def onward(k):
+            zo = zlist[k]
+            nz = jnp.where(zo < z, z + 1, z - 1)
+            ok = (nz >= 0) & (nz < NZ)
+            return zo, nz, ok
+
+        def z_event(k):
+            zo, nz, ok = onward(k)
+            j = index(zo, y, core)
+            arrived(j)
+
+            @pl.when(ok)
+            def _():
+                copy(buf.at[j], j, sz.at[k], index(nz, y, core)).start()
+
+            copy(buf.at[j], j, sy.at[k], across).start()
+            copy(buf.at[j], j, ss.at[k], sibling).start()
+
+        def y_event(k):
+            j = index(zlist[k], 1 - y, core)
+            arrived(j)
+            copy(buf.at[j], j, ss.at[4 + k], sibling).start()
+
+        def finish(src):
+            @pl.when(z < NZ - 1)
+            def _():
+                copy(src, me, sz.at[0], me + 2 * NY).wait_send()
+
+            @pl.when(z > 0)
+            def _():
+                copy(src, me, sz.at[4], me - 2 * NY).wait_send()
+
+            for k in range(1, NZ):
+                zo, nz, ok = onward(k)
+                j = index(zo, y, core)
+
+                @pl.when(ok)
+                def _():
+                    copy(buf.at[j], j, sz.at[k], index(nz, y, core)).wait_send()
+
+            for k in range(NZ):
+                j = index(zlist[k], y, core)
+                copy(src if k == 0 else buf.at[j], j, sy.at[k], across).wait_send()
+                copy(src if k == 0 else buf.at[j], j, ss.at[k], sibling).wait_send()
+                j = index(zlist[k], 1 - y, core)
+                copy(buf.at[j], j, ss.at[4 + k], sibling).wait_send()
+
+        return arrived, start_own, z_event, y_event, finish
+
+    x_arrived, x_own, x_z, x_y, x_finish = relay(xall, recv, send_z, send_y, send_s)
+    a_arrived, a_own, a_z, a_y, a_finish = relay(att, arecv, asend_z, asend_y, asend_s)
+
+    x_own(tok)
+
+    def wcopy(i):
+        d = (me + i) % n
+        return pltpu.make_async_remote_copy(
+            src_ref=wblock(d), dst_ref=wcols.at[me, grp], send_sem=wsend.at[i], recv_sem=wrecv.at[me],
+            device_id={"tensor": d}, device_id_type=MESH,
+        )
+
+    def wstart(i, carry):
+        wcopy(i).start()
+        return carry
+
+    lax.fori_loop(1, n, wstart, 0)
+
+    lanes = lax.broadcasted_iota(jnp.int32, (SEQS, STEPS), 1)
+    onehot = jnp.where(lanes == step[...], 1.0, 0.0).astype(jnp.bfloat16)
+
+    def timed(i, carry):
+        at = pl.ds(pl.multiple_of(i * CHUNK, CHUNK), CHUNK)
+        both = jnp.dot(onehot, table[:, at], preferred_element_type=jnp.float32)
+        for s in range(SEQS):
+            tsc[s, :, at] = both[s : s + 1]
+        return carry
+
+    lax.fori_loop(0, width // CHUNK, timed, 0)
+
+    tall = 2 * rows
+    per_seq = LEN // tall
+
+    def masked_rows(chip):
+        pos = (chip % per_seq) * tall + lax.broadcasted_iota(jnp.int32, (tall, mpos.shape[-1]), 0)
+        hit = jnp.where(pos == mpos[chip // per_seq], 1.0, 0.0)
+        return jnp.max(hit, axis=1, keepdims=True)
+
+    def embedded(chip, hit, at, size):
+        raw = xall[pl.ds(2 * chip, 2), :, at].astype(jnp.float32).reshape(tall, size)
+        base = jnp.where(hit > 0.5, membed[:, at].astype(jnp.float32), raw)
+        return base + tsc[chip // per_seq, :, at]
+
+    def project(chip):
+        hit = masked_rows(chip)
+
+        def squares(i, total):
+            at = pl.ds(pl.multiple_of(i * CHUNK, CHUNK), CHUNK)
+            e = embedded(chip, hit, at, CHUNK)
+            e = e * e
+            for p in range(CHUNK // 128):
+                total = total + e[:, p * 128 : (p + 1) * 128]
+            return total
+
+        total = lax.fori_loop(0, width // CHUNK, squares, jnp.zeros((tall, 128), jnp.float32))
+        scale = lax.rsqrt(jnp.sum(total, axis=1, keepdims=True) / width + 1e-05)
+
+        def multiply(i, total):
+            at = pl.ds(pl.multiple_of(i * CHUNK, CHUNK), CHUNK)
+            normed = (embedded(chip, hit, at, CHUNK) * scale * ngain[:, at]).astype(jnp.bfloat16)
+            return total + jnp.dot(normed, wv[at, :], preferred_element_type=jnp.float32)
+
+        qkv[chip] = lax.fori_loop(
+            0, width // CHUNK, multiply, jnp.zeros((tall, 3 * HEAD_DIM), jnp.float32)
+        )
+
+    def chip_of(k, yy):
+        return zlist[k] * NY + yy
+
+    def attend_one(s):
+        block = qkv[pl.ds(s * per_seq, per_seq)].reshape(LEN, 3 * HEAD_DIM)
+        q = block[:, :HEAD_DIM]
+        k = block[:, HEAD_DIM : 2 * HEAD_DIM]
+        v = block[:, 2 * HEAD_DIM :].astype(jnp.bfloat16)
+        qn = (q * lax.rsqrt(jnp.mean(q * q, axis=1, keepdims=True) + 1e-06) * qkg[0:1, :]).astype(jnp.bfloat16)
+        kn = (k * lax.rsqrt(jnp.mean(k * k, axis=1, keepdims=True) + 1e-06) * qkg[1:2, :]).astype(jnp.bfloat16)
+        scores = lax.dot_general(qn, kn, (((1,), (1,)), ((), ())), preferred_element_type=jnp.float32)
+        weights = jnp.exp(scores * (HEAD_DIM**-0.5))
+        probs = (weights / jnp.sum(weights, axis=1, keepdims=True)).astype(jnp.bfloat16)
+        att[me, pl.ds(pl.multiple_of(s * LEN, LEN), LEN), :] = jnp.dot(
+            probs, v, preferred_element_type=jnp.float32
+        ).astype(jnp.bfloat16)
+
+    inner = (z > 0) & (z < NZ - 1)
+
+    own.wait()
+    for c in wcopies:
+        c.wait()
+    x_arrived(sibling)
+    project(chip_of(0, y))
+    x_z(1)
+
+    @pl.when(inner)
+    def _():
+        x_z(2)
+
+    x_arrived(index(zlist[1], y, 1 - core))
+    project(chip_of(1, y))
+    x_y(0)
+
+    @pl.when(inner)
+    def _():
+        x_z(3)
+
+    x_arrived(index(zlist[0], 1 - y, 1 - core))
+    project(chip_of(0, 1 - y))
+
+    @pl.when(jnp.logical_not(inner))
+    def _():
+        x_z(2)
+
+    x_y(1)
+    x_arrived(index(zlist[1], 1 - y, 1 - core))
+    project(chip_of(1, 1 - y))
+    x_arrived(index(zlist[2], y, 1 - core))
+    project(chip_of(2, y))
+
+    @pl.when(jnp.logical_not(inner))
+    def _():
+        x_z(3)
+
+    attend_one(far)
+    x_y(2)
+    x_arrived(index(zlist[3], y, 1 - core))
+    project(chip_of(3, y))
+    x_arrived(index(zlist[2], 1 - y, 1 - core))
+    project(chip_of(2, 1 - y))
+    x_y(3)
+    x_arrived(index(zlist[3], 1 - y, 1 - core))
+    project(chip_of(3, 1 - y))
+    attend_one(1 - far)
+    a_own(att.at[me])
+
+    wown.wait()
+
+    def wwait(i, carry):
+        j = (me + i) % n
+        pltpu.make_async_remote_copy(
+            src_ref=wcols.at[j, grp], dst_ref=wcols.at[j, grp], send_sem=wsend.at[i], recv_sem=wrecv.at[j],
+            device_id={"tensor": j}, device_id_type=MESH,
+        ).wait_recv()
+        return carry
+
+    lax.fori_loop(1, n, wwait, 0)
+    wshare = pltpu.make_async_remote_copy(
+        src_ref=wcols.at[:, grp], dst_ref=wcols.at[:, grp], send_sem=wx.at[0], recv_sem=wx.at[1],
+        device_id={"groups": 1 - grp}, device_id_type=MESH,
+    )
+    wshare.start()
+    a_z(1)
+
+    @pl.when(inner)
+    def _():
+        a_z(2)
+
+    mine = pl.ds(pl.multiple_of(me * cols, cols), cols)
+
+    def residual(chip, carry):
+        acc[pl.ds(pl.multiple_of(chip * tall, tall), tall), :] = embedded(chip, masked_rows(chip), mine, cols)
+        return carry
+
+    lax.fori_loop(0, SEQS * per_seq, residual, 0)
+
+    @pl.when(jnp.logical_not(inner))
+    def _():
+        a_z(2)
+
+    a_z(3)
+    pltpu.make_async_remote_copy(
+        src_ref=wcols.at[:, 1 - grp], dst_ref=wcols.at[:, 1 - grp], send_sem=wx.at[0], recv_sem=wx.at[1],
+        device_id={"groups": 1 - grp}, device_id_type=MESH,
+    ).wait_recv()
+
+    def head_pair(chip):
+        left = jnp.concatenate([att[2 * chip], att[2 * chip + 1]], axis=1)
+        right = wcols[pl.ds(2 * chip, 2)].reshape(2 * HEAD_DIM, cols)
+        acc[...] += jnp.dot(left, right, preferred_element_type=jnp.float32)
+
+    a_arrived(sibling)
+    head_pair(chip_of(0, y))
+    for k in range(1, NZ):
+        a_y(k - 1)
+        a_arrived(index(zlist[k], y, 1 - core))
+        head_pair(chip_of(k, y))
+    a_y(3)
+    for k in range(NZ):
+        a_arrived(index(zlist[k], 1 - y, 1 - core))
+        head_pair(chip_of(k, 1 - y))
+    out[...] = acc[...].astype(jnp.bfloat16)
+
+    x_finish(tok)
+    a_finish(att.at[me])
+
+    def wdone(i, carry):
+        wcopy(i).wait_send()
+        return carry
+
+    lax.fori_loop(1, n, wdone, 0)
+    wshare.wait_send()
+
+
+def fused(tokens_in, mask_pos, step_index, mask_embed, time_table, norm_gain, w_qkv, qk_gain, w_out):
+    n = lax.axis_size("tensor")
+    rows, width = tokens_in.shape
+    total = n * rows
+    cols = width // n
+    vmem = pl.BlockSpec(memory_space=pltpu.VMEM)
+    hbm = pl.BlockSpec(memory_space=pl.ANY)
+    dma = pltpu.SemaphoreType.DMA
+    return pl.pallas_call(
+        fused_kernel,
+        out_shape=jax.ShapeDtypeStruct((total, cols), jnp.bfloat16),
+        in_specs=[hbm, vmem, vmem, vmem, vmem, vmem, hbm, vmem, hbm],
+        out_specs=vmem,
+        scratch_shapes=[
+            pltpu.VMEM((n, rows, width), jnp.bfloat16),
+            pltpu.VMEM((width, 3 * HEAD_DIM), jnp.bfloat16),
+            pltpu.VMEM((n, 2, HEAD_DIM // 2, cols), jnp.bfloat16),
+            pltpu.VMEM((SEQS, 1, width), jnp.float32),
+            pltpu.VMEM((n // 2, 2 * rows, 3 * HEAD_DIM), jnp.float32),
+            pltpu.VMEM((n, total, HEAD_DIM), jnp.bfloat16),
+            pltpu.VMEM((total, cols), jnp.float32),
+            dma((5,)), dma((n,)), dma((5,)), dma((4,)), dma((8,)), dma((n,)), dma((n,)), dma((2,)),
+            dma((n,)), dma((5,)), dma((4,)), dma((8,)),
+        ],
+        compiler_params=pltpu.CompilerParams(
+            collective_id=0, has_side_effects=True, vmem_limit_bytes=48 * 1024 * 1024
+        ),
+        cost_estimate=pl.CostEstimate(flops=2 * total * width * 3 * HEAD_DIM, bytes_accessed=10 * 1024 * 1024, transcendentals=0),
+    )(
+        tokens_in, mask_pos.reshape(SEQS, 1, -1), step_index.reshape(SEQS, 1), mask_embed.reshape(1, width),
+        time_table, norm_gain.reshape(1, width), w_qkv, qk_gain, w_out,
+    )
+
+
 def solution(mesh):
+    def run(tokens_in, mask_pos, step_index, mask_embed, time_table, norm_gain, w_qkv, qk_gain, w_out):
+        fits = (
+            mesh.shape["tensor"] == 2 * NY * NZ
+            and mesh.shape["groups"] == 2
+            and w_qkv.shape[2] == HEAD_DIM
+            and tokens_in.shape[0] % 16 == 0
+            and tokens_in.shape[0] * mesh.shape["tensor"] == SEQS * LEN
+        )
+        return (fused if fits else body)(
+            tokens_in, mask_pos, step_index, mask_embed, time_table, norm_gain, w_qkv, qk_gain, w_out
+        )
+
     return jax.shard_map(
-        body,
+        run,
         mesh=mesh,
         in_specs=(
             P(("groups", "tensor"), None),

time: 196 us -> 117 us (0.60)
  waiting for transfers between devices: 139 us -> 0 us
  Pallas kernels: 0 us -> 109 us
  matrix products: 24.6 us -> 0 us
  between operations: 13.5 us -> 0.03 us
  starting transfers between devices: 7.46 us -> 0 us
  other arithmetic: 2.39 us -> 0 us
    all_gather x2 -> x0, waiting for transfers between devices: 138 us -> none  [the longest x1 102 us: body(): tokens = lax.all_gather(tokens_in, 'tensor', axis=0, tiled=True)]
    pallas_call x0 -> x1, Pallas kernels: none -> 109 us  [fused(): pl.pallas_call(fused_kernel, out_shape=jax.ShapeDtypeStruct((total, cols)...]
    dot_general x6 -> x0, matrix products: 24.6 us -> none  [the longest x2 8.56 us: embed_rows(): timed = jnp.dot(onehot, table_part, preferred_element_type=jnp.float32)]
    all_to_all x1 -> x0, starting transfers between devices: 7.39 us -> none  [body(): lax.all_to_all(w_out, 'tensor', split_axis=1, concat_axis=0, tiled=True)]
    unnamed x13, local copies, waits for them, and re-layouts: 4.09 us -> 6.76 us
    all_to_all x1 -> x0, local copies, waits for them, and re-layouts: 2.63 us -> none  [body(): lax.all_to_all(w_out, 'tensor', split_axis=1, concat_axis=0, tiled=True)]
  transfers between devices with their start and end apart: 3 -> 0, of which waited for: 2 -> 0; matrix products, arithmetic and copies ran while one was open for 15% -> 0% of each run, Pallas kernels for 0% -> 0%
where the time goes in v2:
time: 117 us
  Pallas kernels  109 us (93%)
  local copies, waits for them, and re-layouts  8.24 us (7%)
    pallas_call x1, Pallas kernels, fused(): pl.pallas_call(fused_kernel, out_shape=jax.ShapeDtypeStruct((total, cols)...  109 us
    unnamed x13, local copies, waits for them, and re-layouts  6.76 us

profile of v2, /device:TPU:0, one launch (start us, length us, event | category | flops | bytes accessed | tf_op | source)
XLA Modules:
  0.0 116.9 jit_solution(8475267947800623443)
XLA Ops:
  0.0 0.7 copy.11.step
  0.7 0.7 reshape.14.membed
  1.5 0.0 copy-start
  1.5 1.6 %copy-done = bf16[128,8192]{1,0:T(8,128)(2,1)S(1)} copy-done((bf16[128,8192]{1,0:T(8,128)(2,1)S(1)}, bf16[128,8192]{1,0:T(8,128)(2,1)}, u32[]{:S(2)}) %copy-start) | copy-done | bytes 2097176
  3.1 0.0 copy-start.1
  3.1 1.2 %copy-done.1 = bf16[64,8192]{1,0:T(8,128)(2,1)S(1)} copy-done((bf16[64,8192]{1,0:T(8,128)(2,1)S(1)}, bf16[64,8192]{1,0:T(8,128)(2,1)}, u32[]{:S(2)}) %copy-start.1) | copy-done | bytes 1048600
  4.3 0.0 copy-start.2
  4.3 1.0 copy-done.2
  5.3 0.0 copy-start.3
  5.3 0.8 copy-done.3
  6.1 0.0 copy-start.4
  6.1 0.7 copy-done.4
  6.8 0.0 copy-start.5
  6.8 0.7 copy-done.5
  7.5 108.6 %shard_map.91 = bf16[512,512]{1,0:T(8,128)(2,1)S(1)} custom-call(bf16[32,8192]{1,0:T(8,128)(2,1)S(1)} %copy-done.2, s32[2,1,64]{2,1,0:T(1,128)S(1)} %bitcast.6, s32[2,1]{1,0:T(2,128)S(1)} %copy.11.step, bf16[1,8192]{1,0:T(2,128)(2,1)S(1)} %reshape.14.membed, bf16[64,8192]{1,0:T(8,128)(2,1)S(1)} %copy-done.1, f32[1,8192]{1,0:T(1,128)S(1)} %bitcast.5, ...), custom_call_target="tpu_custom_call" | custom-call | flops 3221225472 | bytes 10485760 | tf_op jit(solution)/shard_map/pallas_call | solution.py:422
  116.1 0.8 copy.13
Async XLA Ops:
  1.5 1.6 %copy-start = (bf16[128,8192]{1,0:T(8,128)(2,1)S(1)}, bf16[128,8192]{1,0:T(8,128)(2,1)}, u32[]{:S(2)}) copy-start(bf16[128,8192]{1,0:T(8,128)(2,1)} %wout.1) | copy-start | bytes 6291460
  3.1 1.2 %copy-start.1 = (bf16[64,8192]{1,0:T(8,128)(2,1)S(1)}, bf16[64,8192]{1,0:T(8,128)(2,1)}, u32[]{:S(2)}) copy-start(bf16[64,8192]{1,0:T(8,128)(2,1)} %table.1) | copy-start | bytes 3145732
  4.3 1.0 copy-start.2
  5.3 0.8 copy-start.3
  6.1 0.7 copy-start.4
  6.8 0.7 copy-start.5

commit v3 on v2

--- a/solution.py
+++ b/solution.py
@@ -93,9 +93,9 @@
 
 
 def fused_kernel(
-    tok, mpos, step, membed, table, ngain, wqkv, qkg, wout, out,
-    xall, wv, wcols, tsc, qkv, att, acc,
-    loc, recv, send_z, send_y, send_s, wsend, wrecv, wx, arecv, asend_z, asend_y, asend_s,
+    tok, mpos_h, step, membed_h, table_h, ngain_h, wqkv, qkg_h, wout, out,
+    mpos, membed, table, ngain, qkg, xall, wv, wcols, tsc, qkv, att, acc,
+    loc, recv, send_z, send_y, send_s, wsend, wrecv, wx_s, wx_r, arecv, asend_z, asend_y, asend_s, brecv, bsend_z, bsend_y, bsend_s,
 ):
     n, rows, width = xall.shape
     cols = width // n
@@ -129,6 +129,15 @@
     wown = pltpu.make_async_copy(wblock(me), wcols.at[me, grp], loc.at[4])
     wown.start()
 
+    small = [
+        pltpu.make_async_copy(src, dst, loc.at[5 + i])
+        for i, (src, dst) in enumerate(
+            [(mpos_h, mpos), (membed_h, membed), (table_h, table), (ngain_h, ngain), (qkg_h, qkg)]
+        )
+    ]
+    for c in small:
+        c.start()
+
     barrier = pltpu.get_barrier_semaphore()
 
     def greet(i, carry):
@@ -139,15 +148,15 @@
     pl.semaphore_signal(barrier, inc=1, device_id={"groups": 1 - grp}, device_id_type=MESH)
     pl.semaphore_wait(barrier, n)
 
-    def relay(buf, rsem, sz, sy, ss):
+    def relay(slot, rsem, sz, sy, ss):
         def copy(src, j, sem, to):
             return pltpu.make_async_remote_copy(
-                src_ref=src, dst_ref=buf.at[j], send_sem=sem, recv_sem=rsem.at[j],
+                src_ref=src, dst_ref=slot(j), send_sem=sem, recv_sem=rsem.at[j],
                 device_id={"tensor": to}, device_id_type=MESH,
             )
 
         def arrived(j):
-            copy(buf.at[j], j, sy.at[0], sibling).wait_recv()
+            copy(slot(j), j, sy.at[0], sibling).wait_recv()
 
         def start_own(src):
             @pl.when(z < NZ - 1)
@@ -174,15 +183,15 @@
 
             @pl.when(ok)
             def _():
-                copy(buf.at[j], j, sz.at[k], index(nz, y, core)).start()
-
-            copy(buf.at[j], j, sy.at[k], across).start()
-            copy(buf.at[j], j, ss.at[k], sibling).start()
+                copy(slot(j), j, sz.at[k], index(nz, y, core)).start()
+
+            copy(slot(j), j, sy.at[k], across).start()
+            copy(slot(j), j, ss.at[k], sibling).start()
 
         def y_event(k):
             j = index(zlist[k], 1 - y, core)
             arrived(j)
-            copy(buf.at[j], j, ss.at[4 + k], sibling).start()
+            copy(slot(j), j, ss.at[4 + k], sibling).start()
 
         def finish(src):
             @pl.when(z < NZ - 1)
@@ -199,19 +208,28 @@
 
                 @pl.when(ok)
                 def _():
-                    copy(buf.at[j], j, sz.at[k], index(nz, y, core)).wait_send()
+                    copy(slot(j), j, sz.at[k], index(nz, y, core)).wait_send()
 
             for k in range(NZ):
                 j = index(zlist[k], y, core)
-                copy(src if k == 0 else buf.at[j], j, sy.at[k], across).wait_send()
-                copy(src if k == 0 else buf.at[j], j, ss.at[k], sibling).wait_send()
+                copy(src if k == 0 else slot(j), j, sy.at[k], across).wait_send()
+                copy(src if k == 0 else slot(j), j, ss.at[k], sibling).wait_send()
                 j = index(zlist[k], 1 - y, core)
-                copy(buf.at[j], j, ss.at[4 + k], sibling).wait_send()
+                copy(slot(j), j, ss.at[4 + k], sibling).wait_send()
 
         return arrived, start_own, z_event, y_event, finish
 
-    x_arrived, x_own, x_z, x_y, x_finish = relay(xall, recv, send_z, send_y, send_s)
-    a_arrived, a_own, a_z, a_y, a_finish = relay(att, arecv, asend_z, asend_y, asend_s)
+    def part(first):
+        def slot(j):
+            s = (j // (2 * NY)) // 2
+            s = s if first else 1 - s
+            return att.at[j, pl.ds(pl.multiple_of(s * LEN, LEN), LEN)]
+
+        return slot
+
+    x_arrived, x_own, x_z, x_y, x_finish = relay(lambda j: xall.at[j], recv, send_z, send_y, send_s)
+    a_arrived, a_own, a_z, a_y, a_finish = relay(part(True), arecv, asend_z, asend_y, asend_s)
+    b_arrived, b_own, b_z, b_y, b_finish = relay(part(False), brecv, bsend_z, bsend_y, bsend_s)
 
     x_own(tok)
 
@@ -226,10 +244,13 @@
         wcopy(i).start()
         return carry
 
-    lax.fori_loop(1, n, wstart, 0)
+    for c in small:
+        c.wait()
 
     lanes = lax.broadcasted_iota(jnp.int32, (SEQS, STEPS), 1)
-    onehot = jnp.where(lanes == step[...], 1.0, 0.0).astype(jnp.bfloat16)
+    which = lax.broadcasted_iota(jnp.int32, (SEQS, STEPS), 0)
+    chosen = jnp.where(which == 0, step[0], step[1])
+    onehot = jnp.where(lanes == chosen, 1.0, 0.0).astype(jnp.bfloat16)
 
     def timed(i, carry):
         at = pl.ds(pl.multiple_of(i * CHUNK, CHUNK), CHUNK)
@@ -321,9 +342,12 @@
     def _():
         x_z(2)
 
+    lax.fori_loop(1, n, wstart, 0)
     x_y(1)
     x_arrived(index(zlist[1], 1 - y, 1 - core))
     project(chip_of(1, 1 - y))
+    attend_one(far)
+    a_own(part(True)(me))
     x_arrived(index(zlist[2], y, 1 - core))
     project(chip_of(2, y))
 
@@ -331,40 +355,67 @@
     def _():
         x_z(3)
 
-    attend_one(far)
     x_y(2)
     x_arrived(index(zlist[3], y, 1 - core))
     project(chip_of(3, y))
+    a_z(1)
+
+    @pl.when(inner)
+    def _():
+        a_z(2)
+
+    wown.wait()
+
+    def wshare(zz, own_half):
+        blocks = pl.ds(2 * NY * zz, 2 * NY)
+        g = grp if own_half else 1 - grp
+        return pltpu.make_async_remote_copy(
+            src_ref=wcols.at[blocks, g], dst_ref=wcols.at[blocks, g], send_sem=wx_s.at[zz], recv_sem=wx_r.at[zz],
+            device_id={"groups": 1 - grp}, device_id_type=MESH,
+        )
+
+    def share(zz):
+        def wwait(i, carry):
+            j = 2 * NY * zz + i
+
+            @pl.when(j != me)
+            def _():
+                pltpu.make_async_remote_copy(
+                    src_ref=wcols.at[j, grp], dst_ref=wcols.at[j, grp], send_sem=wsend.at[i], recv_sem=wrecv.at[j],
+                    device_id={"tensor": sibling}, device_id_type=MESH,
+                ).wait_recv()
+
+            return carry
+
+        lax.fori_loop(0, 2 * NY, wwait, 0)
+        wshare(zz, True).start()
+
+    share(zlist[0])
     x_arrived(index(zlist[2], 1 - y, 1 - core))
     project(chip_of(2, 1 - y))
+
+    @pl.when(jnp.logical_not(inner))
+    def _():
+        a_z(2)
+
+    a_z(3)
+    share(zlist[1])
     x_y(3)
     x_arrived(index(zlist[3], 1 - y, 1 - core))
     project(chip_of(3, 1 - y))
     attend_one(1 - far)
-    a_own(att.at[me])
-
-    wown.wait()
-
-    def wwait(i, carry):
-        j = (me + i) % n
-        pltpu.make_async_remote_copy(
-            src_ref=wcols.at[j, grp], dst_ref=wcols.at[j, grp], send_sem=wsend.at[i], recv_sem=wrecv.at[j],
-            device_id={"tensor": j}, device_id_type=MESH,
-        ).wait_recv()
-        return carry
-
-    lax.fori_loop(1, n, wwait, 0)
-    wshare = pltpu.make_async_remote_copy(
-        src_ref=wcols.at[:, grp], dst_ref=wcols.at[:, grp], send_sem=wx.at[0], recv_sem=wx.at[1],
-        device_id={"groups": 1 - grp}, device_id_type=MESH,
-    )
-    wshare.start()
-    a_z(1)
+    b_own(part(False)(me))
+    for k in range(NZ):
+        a_y(k)
+    share(zlist[2])
+    b_z(1)
 
     @pl.when(inner)
     def _():
-        a_z(2)
-
+        b_z(2)
+
+    share(zlist[3])
+    b_y(0)
     mine = pl.ds(pl.multiple_of(me * cols, cols), cols)
 
     def residual(chip, carry):
@@ -375,40 +426,48 @@
 
     @pl.when(jnp.logical_not(inner))
     def _():
-        a_z(2)
-
-    a_z(3)
-    pltpu.make_async_remote_copy(
-        src_ref=wcols.at[:, 1 - grp], dst_ref=wcols.at[:, 1 - grp], send_sem=wx.at[0], recv_sem=wx.at[1],
-        device_id={"groups": 1 - grp}, device_id_type=MESH,
-    ).wait_recv()
+        b_z(2)
+
+    b_z(3)
+    b_y(1)
 
     def head_pair(chip):
         left = jnp.concatenate([att[2 * chip], att[2 * chip + 1]], axis=1)
         right = wcols[pl.ds(2 * chip, 2)].reshape(2 * HEAD_DIM, cols)
         acc[...] += jnp.dot(left, right, preferred_element_type=jnp.float32)
 
-    a_arrived(sibling)
-    head_pair(chip_of(0, y))
-    for k in range(1, NZ):
-        a_y(k - 1)
-        a_arrived(index(zlist[k], y, 1 - core))
-        head_pair(chip_of(k, y))
-    a_y(3)
-    for k in range(NZ):
-        a_arrived(index(zlist[k], 1 - y, 1 - core))
-        head_pair(chip_of(k, 1 - y))
+    def ready(k, yy):
+        a_arrived(index(zlist[k], yy, 1 - core))
+        b_arrived(index(zlist[k], yy, 1 - core))
+        head_pair(chip_of(k, yy))
+
+    wshare(zlist[0], False).wait_recv()
+    ready(0, y)
+    ready(0, 1 - y)
+    wshare(zlist[1], False).wait_recv()
+    ready(1, y)
+    b_y(2)
+    ready(1, 1 - y)
+    wshare(zlist[2], False).wait_recv()
+    ready(2, y)
+    b_y(3)
+    wshare(zlist[3], False).wait_recv()
+    ready(3, y)
+    ready(2, 1 - y)
+    ready(3, 1 - y)
     out[...] = acc[...].astype(jnp.bfloat16)
 
     x_finish(tok)
-    a_finish(att.at[me])
+    a_finish(part(True)(me))
+    b_finish(part(False)(me))
 
     def wdone(i, carry):
         wcopy(i).wait_send()
         return carry
 
     lax.fori_loop(1, n, wdone, 0)
-    wshare.wait_send()
+    for zz in range(NZ):
+        wshare(zz, True).wait_send()
 
 
 def fused(tokens_in, mask_pos, step_index, mask_embed, time_table, norm_gain, w_qkv, qk_gain, w_out):
@@ -422,9 +481,14 @@
     return pl.pallas_call(
         fused_kernel,
         out_shape=jax.ShapeDtypeStruct((total, cols), jnp.bfloat16),
-        in_specs=[hbm, vmem, vmem, vmem, vmem, vmem, hbm, vmem, hbm],
+        in_specs=[hbm, hbm, pl.BlockSpec(memory_space=pltpu.SMEM)] + [hbm] * 6,
         out_specs=vmem,
         scratch_shapes=[
+            pltpu.VMEM((SEQS, 1, mask_pos.shape[1]), jnp.int32),
+            pltpu.VMEM((1, width), jnp.bfloat16),
+            pltpu.VMEM(time_table.shape, jnp.bfloat16),
+            pltpu.VMEM((1, width), jnp.float32),
+            pltpu.VMEM(qk_gain.shape, jnp.float32),
             pltpu.VMEM((n, rows, width), jnp.bfloat16),
             pltpu.VMEM((width, 3 * HEAD_DIM), jnp.bfloat16),
             pltpu.VMEM((n, 2, HEAD_DIM // 2, cols), jnp.bfloat16),
@@ -432,15 +496,15 @@
             pltpu.VMEM((n // 2, 2 * rows, 3 * HEAD_DIM), jnp.float32),
             pltpu.VMEM((n, total, HEAD_DIM), jnp.bfloat16),
             pltpu.VMEM((total, cols), jnp.float32),
-            dma((5,)), dma((n,)), dma((5,)), dma((4,)), dma((8,)), dma((n,)), dma((n,)), dma((2,)),
-            dma((n,)), dma((5,)), dma((4,)), dma((8,)),
+            dma((10,)), dma((n,)), dma((5,)), dma((4,)), dma((8,)), dma((n,)), dma((n,)), dma((4,)), dma((4,)),
+            dma((n,)), dma((5,)), dma((4,)), dma((8,)), dma((n,)), dma((5,)), dma((4,)), dma((8,)),
         ],
         compiler_params=pltpu.CompilerParams(
             collective_id=0, has_side_effects=True, vmem_limit_bytes=48 * 1024 * 1024
         ),
         cost_estimate=pl.CostEstimate(flops=2 * total * width * 3 * HEAD_DIM, bytes_accessed=10 * 1024 * 1024, transcendentals=0),
     )(
-        tokens_in, mask_pos.reshape(SEQS, 1, -1), step_index.reshape(SEQS, 1), mask_embed.reshape(1, width),
+        tokens_in, mask_pos.reshape(SEQS, 1, -1), step_index, mask_embed.reshape(1, width),
         time_table, norm_gain.reshape(1, width), w_qkv, qk_gain, w_out,
     )
 

time: 117 us -> 102 us (0.87)
  Pallas kernels: 109 us -> 93.7 us
    pallas_call x1, Pallas kernels: 109 us -> 93.7 us  [fused(): pl.pallas_call(fused_kernel, out_shape=jax.ShapeDtypeStruct((total, cols)...]
    unnamed x13 -> x15, local copies, waits for them, and re-layouts: 6.76 us -> 7.42 us
where the time goes in v3:
time: 102 us
  Pallas kernels  93.7 us (92%)
  local copies, waits for them, and re-layouts  8.15 us (8%)
    pallas_call x1, Pallas kernels, fused(): pl.pallas_call(fused_kernel, out_shape=jax.ShapeDtypeStruct((total, cols)...  93.7 us
    unnamed x15, local copies, waits for them, and re-layouts  7.42 us

profile of v3, /device:TPU:0, one launch (start us, length us, event | category | flops | bytes accessed | tf_op | source)
XLA Modules:
  0.0 101.9 jit_solution(1240182000313757052)
XLA Ops:
  0.0 0.7 reshape.10.membed_h
  0.7 0.0 copy-start
  0.8 1.6 %copy-done = bf16[128,8192]{1,0:T(8,128)(2,1)S(1)} copy-done((bf16[128,8192]{1,0:T(8,128)(2,1)S(1)}, bf16[128,8192]{1,0:T(8,128)(2,1)}, u32[]{:S(2)}) %copy-start) | copy-done | bytes 2097176
  2.3 0.0 copy-start.1
  2.3 1.2 %copy-done.1 = bf16[64,8192]{1,0:T(8,128)(2,1)S(1)} copy-done((bf16[64,8192]{1,0:T(8,128)(2,1)S(1)}, bf16[64,8192]{1,0:T(8,128)(2,1)}, u32[]{:S(2)}) %copy-start.1) | copy-done | bytes 1048600
  3.6 0.0 copy-start.2
  3.6 1.0 %copy-done.2 = bf16[32,8192]{1,0:T(8,128)(2,1)S(1)} copy-done((bf16[32,8192]{1,0:T(8,128)(2,1)S(1)}, bf16[32,8192]{1,0:T(8,128)(2,1)}, u32[]{:S(2)}) %copy-start.2) | copy-done | bytes 524312
  4.6 0.0 copy-start.3
  4.6 0.8 copy-done.3
  5.4 0.0 copy-start.4
  5.4 0.7 copy-done.4
  6.0 0.0 copy-start.5
  6.0 0.7 copy-done.5
  6.7 0.0 copy-start.6
  6.7 0.7 copy-done.6
  7.4 93.7 %shard_map.91 = bf16[512,512]{1,0:T(8,128)(2,1)S(1)} custom-call(bf16[32,8192]{1,0:T(8,128)(2,1)S(1)} %copy-done.2, s32[2,1,64]{2,1,0:T(1,128)S(1)} %bitcast.5, s32[2]{0:T(128)S(1)} %copy-done.6, bf16[1,8192]{1,0:T(2,128)(2,1)S(1)} %reshape.10.membed_h, bf16[64,8192]{1,0:T(8,128)(2,1)S(1)} %copy-done.1, f32[1,8192]{1,0:T(1,128)S(1)} %bitcast.4, ...), custom_call_target="tpu_custom_call" | custom-call | flops 3221225472 | bytes 10485760 | tf_op jit(solution)/shard_map/pallas_call | solution.py:481
  101.1 0.8 copy.12
Async XLA Ops:
  0.7 1.6 %copy-start = (bf16[128,8192]{1,0:T(8,128)(2,1)S(1)}, bf16[128,8192]{1,0:T(8,128)(2,1)}, u32[]{:S(2)}) copy-start(bf16[128,8192]{1,0:T(8,128)(2,1)} %wout.1) | copy-start | bytes 6291460
  2.3 1.2 %copy-start.1 = (bf16[64,8192]{1,0:T(8,128)(2,1)S(1)}, bf16[64,8192]{1,0:T(8,128)(2,1)}, u32[]{:S(2)}) copy-start(bf16[64,8192]{1,0:T(8,128)(2,1)} %table_h.1) | copy-start | bytes 3145732
  3.6 1.0 %copy-start.2 = (bf16[32,8192]{1,0:T(8,128)(2,1)S(1)}, bf16[32,8192]{1,0:T(8,128)(2,1)}, u32[]{:S(2)}) copy-start(bf16[32,8192]{1,0:T(8,128)(2,1)} %tok.1) | copy-start | bytes 1572868
  4.6 0.8 copy-start.3
  5.4 0.7 copy-start.4
  6.0 0.7 copy-start.5
  6.7 0.7 copy-start.6
